TPU v7x, 32 devices: a whole 2x2x4 slice. The times are simulated.
32 devices in a mesh: seq: 32 (over z, y, x, core).
Axes of the slice: x: 2, y: 2, z: 4, core: 2. Of those that a mesh axis runs over, the one named last changes fastest.
Arguments:
- tokens: bfloat16 [8192, 768], P('seq'), may hold values from -64 to 64
- w_query: bfloat16 [768, 768], replicated, may hold values from -0.21875 to 0.21875
- w_key: bfloat16 [768, 768], replicated, may hold values from -0.21875 to 0.21875
- w_value: bfloat16 [768, 768], replicated, may hold values from -0.21875 to 0.21875
- w_out: bfloat16 [768, 768], replicated, may hold values from -0.21875 to 0.21875
- ln_gain: float32 [768], replicated, may hold values from 0.5 to 1.5
- ln_bias: float32 [768], replicated, may hold values from -3 to 3
Outputs:
- encoded: bfloat16 [8192, 768], P('seq')
All inputs are finite; a program needn't handle non-finite values.
Results may differ from a plain program's by a relative error of at most 0.003.
The roundings to bfloat16 on the way count: a program that leaves them out, or rounds other values in their place, can miss the bound.
Values may be sent and summed in bfloat16 or wider, within the bound.
A program may use at most 256 MiB of HBM per device.

v0:
```python
import math

import jax
import jax.numpy as jnp
from jax import lax
from jax.sharding import PartitionSpec as P

H = 12
BLOCK = 64
NG = 128


def broadcast(block, axis, holder):
    block = jnp.where(lax.axis_index(axis) == holder, block, jnp.zeros_like(block))
    return lax.psum(block, axis)


def with_halo(cells, sides, width):
    for axis, dim in sides:
        count = lax.axis_size(axis)
        ends = count - 1
        head = lax.slice_in_dim(cells, 0, width, axis=dim)
        tail = lax.slice_in_dim(cells, cells.shape[dim] - width, cells.shape[dim], axis=dim)
        cells = jnp.concatenate(
            [
                lax.ppermute(tail, axis, [(i, (i + 1) % count) for i in range(ends)]),
                cells,
                lax.ppermute(head, axis, [((i + 1) % count, i) for i in range(ends)]),
            ],
            axis=dim,
        )
    return cells


def project(inputs, weight):
    return jnp.dot(inputs, weight, preferred_element_type=jnp.float32).astype(jnp.bfloat16)


def layer_norm(summed, ln_gain, ln_bias):
    center = summed - jnp.mean(summed, axis=-1, keepdims=True)
    spread = jnp.mean(center * center, axis=-1, keepdims=True)
    return center * lax.rsqrt(spread + 1e-05) * ln_gain + ln_bias


def shards(tokens, w_query, w_key, w_value, w_out, ln_gain, ln_bias):
    local_rows = tokens.shape[0]
    model_width = tokens.shape[1]
    head_count = H
    head_dim = model_width // head_count
    scale_factor = 1.0 / math.sqrt(head_dim)
    shard_count = lax.axis_size("seq")
    device_index = lax.axis_index("seq")
    first_row = device_index * local_rows
    seq_total = local_rows * shard_count
    query_rows = project(tokens, w_query)
    key_rows = project(tokens, w_key)
    value_rows = project(tokens, w_value)
    leading = jnp.stack([query_rows[:NG], key_rows[:NG], value_rows[:NG]], axis=0)
    shared = broadcast(leading, "seq", 0)
    global_queries = shared[0]
    global_keys = shared[1]
    global_values = shared[2]
    stacked = jnp.stack([key_rows, value_rows], axis=1)
    extended = with_halo(stacked, (("seq", 0),), BLOCK)
    wide_keys = extended[:, 0]
    wide_values = extended[:, 1]
    global_key_grid = global_keys.reshape(NG, head_count, head_dim)
    global_value_grid = global_values.reshape(NG, head_count, head_dim)
    block_count = query_rows.shape[0] // BLOCK
    query_grid = query_rows.reshape(block_count, BLOCK, head_count, head_dim)
    key_grid = wide_keys.reshape(block_count + 2, BLOCK, head_count, head_dim)
    value_grid = wide_values.reshape(block_count + 2, BLOCK, head_count, head_dim)
    global_key_rep = jnp.broadcast_to(
        global_key_grid[None], (block_count, NG, head_count, head_dim)
    )
    global_value_rep = jnp.broadcast_to(
        global_value_grid[None], (block_count, NG, head_count, head_dim)
    )
    key_window = jnp.concatenate(
        [key_grid[:-2], key_grid[1:-1], key_grid[2:], global_key_rep], axis=1
    )
    value_window = jnp.concatenate(
        [value_grid[:-2], value_grid[1:-1], value_grid[2:], global_value_rep], axis=1
    )
    joint_scores = (
        jnp.einsum("nqhd,nkhd->nhqk", query_grid, key_window, preferred_element_type=jnp.float32)
        * scale_factor
    )
    positions = (
        first_row
        - BLOCK
        + jnp.arange(block_count, dtype=jnp.int32)[:, None] * BLOCK
        + jnp.arange(3 * BLOCK, dtype=jnp.int32)[None, :]
    )
    usable = jnp.concatenate(
        [(positions >= NG) & (positions < seq_total), jnp.ones((block_count, NG), bool)], axis=1
    )
    joint_scores = jnp.where(usable[:, None, None, :], joint_scores, -jnp.inf)
    row_top = jnp.max(joint_scores, axis=-1, keepdims=True)
    joint_exp = jnp.exp(joint_scores - row_top)
    row_total = jnp.sum(joint_exp, axis=-1)
    blended = jnp.einsum(
        "nhqk,nkhd->nqhd",
        joint_exp.astype(jnp.bfloat16),
        value_window,
        preferred_element_type=jnp.float32,
    )
    blended = blended / jnp.transpose(row_total, (0, 2, 1))[..., None]
    window_out = blended.reshape(block_count * BLOCK, model_width)
    global_query_grid = global_queries.reshape(NG, head_count, head_dim)
    local_scores = (
        jnp.einsum(
            "ghd,jhd->hgj",
            global_query_grid,
            key_rows.reshape(local_rows, head_count, head_dim),
            preferred_element_type=jnp.float32,
        )
        * scale_factor
    )
    local_top = jnp.max(local_scores, axis=-1)
    local_exp = jnp.exp(local_scores - local_top[..., None])
    local_total = jnp.sum(local_exp, axis=-1)
    local_acc = jnp.einsum(
        "hgj,jhd->ghd",
        local_exp.astype(jnp.bfloat16),
        value_rows.reshape(local_rows, head_count, head_dim),
        preferred_element_type=jnp.float32,
    ).reshape(NG, model_width)

    def rescale(weighted, factors):
        return (
            weighted.reshape(NG, head_count, head_dim) * jnp.transpose(factors)[..., None]
        ).reshape(NG, model_width)

    full_top = lax.pmax(local_top, "seq")
    shrink = jnp.exp(local_top - full_top)
    full_total, full_acc = lax.psum((local_total * shrink, rescale(local_acc, shrink)), "seq")
    global_out = rescale(full_acc, 1.0 / full_total)
    row_ids = jnp.arange(local_rows, dtype=jnp.int32)[:, None]
    owner_rows = (row_ids < NG) & (device_index == 0)
    padded = jnp.concatenate(
        [global_out, jnp.zeros((local_rows - NG, model_width), jnp.float32)], axis=0
    )
    attended = jnp.where(owner_rows, padded, window_out).astype(jnp.bfloat16)
    projected = jnp.dot(attended, w_out, preferred_element_type=jnp.float32)
    summed = tokens.astype(jnp.float32) + projected
    return layer_norm(summed, ln_gain, ln_bias).astype(jnp.bfloat16)


def solution(mesh):
    in_specs = (P("seq", None), P(), P(), P(), P(), P(), P())
    out_specs = P("seq", None)
    return jax.shard_map(shards, mesh=mesh, in_specs=in_specs, out_specs=out_specs, check_vma=False)
```

profile of v0, /device:TPU:0, one launch (start us, length us, event | category | flops | bytes accessed | tf_op | source)
XLA Modules:
  0.0 327.5 jit_solution(10396720905622950666)
XLA Ops:
  6.6 2.0 convolution_convert_fusion
  8.6 1.9 convolution_convert_fusion.2
  11.8 0.9 maximum_select_fusion
  13.5 3.0 collective-permute-start
  16.5 1.3 collective-permute-start.1
  17.9 0.9 copy.22
  18.8 0.9 copy.20
  20.4 2.4 reshape.70
  22.8 1.6 reshape.68
  24.4 1.6 copy.36
  26.0 2.5 copy.28
  29.7 2.0 pad_maximum_fusion.5
  31.7 1.7 reshape.71
  33.4 1.6 copy.35
  34.9 1.7 reshape.73
  36.6 1.5 copy.37
  38.8 1.5 copy.27
  40.9 1.5 copy.29
  42.5 100.2 %all-reduce.5.cloned.1.call-done = bf16[3,128,768]{2,1,0:T(8,128)(2,1)} async-done(((bf16[3,128,768]{2,1,0:T(8,128)(2,1)}), bf16[3,128,768]{2,1,0:T(8,128)(2,1)}) %all-reduce.5.cloned.1.call-update) | async-done | bytes 589840 | tf_op jit(solution)/shard_map/psum | solution.py:15
  142.7 1.9 fusion.45
  145.4 1.6 fusion.46
  147.0 40.5 %pmax.7 = f32[12,128]{1,0:T(8,128)} all-reduce(f32[12,128]{1,0:T(8,128)S(1)} %get-tuple-element.20), channel_id=1, replica_groups=mesh['seq'=32] {'seq'}, use_global_device_ids=true, to_apply=%region_2.3 | all-reduce | flops 1536 | bytes 12288 | tf_op jit(solution)/shard_map/pmax | solution.py:135
  188.7 1.2 fusion.30
  190.0 40.7 %psum.23 = f32[12,128]{1,0:T(8,128)S(1)} all-reduce(f32[12,128]{1,0:T(8,128)S(1)} %get-tuple-element.16), channel_id=1, replica_groups=mesh['seq'=32] {'seq'}, use_global_device_ids=true, to_apply=%region_5.6 | all-reduce | flops 1536 | bytes 12288 | tf_op jit(solution)/shard_map/psum | solution.py:137
  230.7 1.1 copy.34
  231.8 1.1 copy.26
  233.1 4.2 %fusion = (f32[4,12,64]{2,1,0:T(8,128)S(1)}, f32[4,12,64,320]{3,2,1,0:T(8,128)S(1)}) fusion(pred[4,320]{1,0:T(4,128)(4,1)} %concatenate.25, bf16[4,128,12,64]{1,3,2,0:T(8,128)(2,1)S(1)} %broadcast_in_dim.58, bf16[4,64,12,64]{1,3,2,0:T(8,128)(2,1)} %copy.37, bf16[4,64,12,64]{1,3,2,0:T(8,128)(2,1)} %copy.36, bf16[4,64,12,64]{1,3,2,0:T(8,128)(2,1)} %copy.35, ...), kind=kOutput, calls=%fused_computation.2 | convolution fusion | flops 136639488 | bytes 6305024 | tf_op jit(solution)/shard_map/nqhd,nkhd->nhqk/dot_general | solution.py:86
  237.3 1.4 fusion.1
  238.9 3.1 bitcast_divide_fusion
  243.2 74.6 %all-reduce.7.cloned.1.call-done = f32[128,768]{0,1:T(8,128)} async-done(((f32[128,768]{0,1:T(8,128)}), f32[128,768]{0,1:T(8,128)}) %all-reduce.7.cloned.1.call-update) | async-done | bytes 393232 | tf_op jit(solution)/shard_map/psum | solution.py:137
  317.8 1.0 bitcast_multiply_fusion
  319.7 0.9 add_convert_fusion
  (53 shorter events, 9.6 us)
Async XLA Ops:
  6.5 312.3 %copy-start = (bf16[768,768]{1,0:T(8,128)(2,1)S(1)}, bf16[768,768]{1,0:T(8,128)(2,1)}, u32[]{:S(2)}) copy-start(bf16[768,768]{1,0:T(8,128)(2,1)} %param.11) | copy-start | bytes 3538948
  6.5 3.9 %copy-start.1 = (bf16[256,768]{1,0:T(8,128)(2,1)S(1)}, bf16[256,768]{1,0:T(8,128)(2,1)}, u32[]{:S(2)}) copy-start(bf16[256,768]{1,0:T(8,128)(2,1)} %param.7) | copy-start | bytes 1179652
  6.5 3.9 %copy-start.4 = (bf16[768,768]{1,0:T(8,128)(2,1)S(1)}, bf16[768,768]{1,0:T(8,128)(2,1)}, u32[]{:S(2)}) copy-start(bf16[768,768]{1,0:T(8,128)(2,1)} %param.8) | copy-start | bytes 3538948
  6.5 136.1 %all-reduce.5.cloned.1.call-start = ((), (), s32[]{:S(2)}) async-start(), calls=%async_computation | async-start | bytes 1179648 | tf_op jit(solution)/shard_map/psum | solution.py:15
  11.0 0.7 copy-start.2
  12.7 305.1 %all-reduce.7.cloned.1.call-start = ((), (), s32[]{:S(2)}) async-start(), calls=%async_computation.1 | async-start | bytes 786432 | tf_op jit(solution)/shard_map/psum | solution.py:137
  13.5 16.2 %collective-permute-start = (bf16[64,2,768]{2,0,1:T(8,128)(2,1)}, bf16[64,2,768]{2,0,1:T(8,128)(2,1)}, u32[]{:S(2)}, u32[]{:S(2)}) collective-permute-start(bf16[64,2,768]{2,0,1:T(8,128)(2,1)} %get-tuple-element.11), channel_id=1, source_target_pairs={{0,1},{1,2},{2,3},{3,4},{4,5},{5,6},{6,7},{7,8},{8,9},{9,10},{10,1... | collective-permute-start | bytes 589832 | tf_op jit(solution)/shard_map/ppermute | solution.py:26
  16.5 13.1 %collective-permute-start.1 = (bf16[64,2,768]{2,0,1:T(8,128)(2,1)}, bf16[64,2,768]{2,0,1:T(8,128)(2,1)}, u32[]{:S(2)}, u32[]{:S(2)}) collective-permute-start(bf16[64,2,768]{2,0,1:T(8,128)(2,1)} %get-tuple-element.12), channel_id=1, source_target_pairs={{1,0},{2,1},{3,2},{4,3},{5,4},{6,5},{7,6},{8,7},{9,8},{10,9},{11,1... | collective-permute-start | bytes 589832 | tf_op jit(solution)/shard_map/ppermute | solution.py:28
  144.6 44.2 %copy-start.3 = (bf16[256,768]{0,1:T(8,128)(2,1)S(1)}, bf16[256,768]{0,1:T(8,128)(2,1)}, u32[]{:S(2)}) copy-start(bf16[256,768]{0,1:T(8,128)(2,1)} %copy.20) | copy-start | bytes 1179652
  233.1 4.2 %copy-start.8 = (pred[4,320]{1,0:T(4,128)(4,1)S(1)}, pred[4,320]{1,0:T(4,128)(4,1)}, u32[]{:S(2)}) copy-start(pred[4,320]{1,0:T(4,128)(4,1)} %concatenate.25) | copy-start | bytes 3844
  237.3 1.7 copy-start.5
  237.3 1.7 copy-start.6
  237.3 1.7 copy-start.7
  242.0 76.8 %copy-start.11 = (pred[256]{0:T(512)(128)(4,1)S(1)}, pred[256]{0:T(512)(128)(4,1)}, u32[]{:S(2)}) copy-start(pred[256]{0:T(512)(128)(4,1)} %compare_and_fusion) | copy-start | bytes 772
  243.1 76.6 %copy-start.9 = (f32[768]{0:T(1024)S(1)}, f32[768]{0:T(1024)}, u32[]{:S(2)}) copy-start(f32[768]{0:T(1024)} %param.13) | copy-start | bytes 9220
  243.1 76.5 %copy-start.10 = (f32[768]{0:T(1024)S(1)}, f32[768]{0:T(1024)}, u32[]{:S(2)}) copy-start(f32[768]{0:T(1024)} %param.12) | copy-start | bytes 9220
Sparse Core Ops, SparseCore 0:
  12.8 129.8 all-reduce.4
  190.1 127.6 all-reduce.6
where the time goes:
time: 328 us; the launch traced here: 327 us
  waiting for transfers between devices  175 us (53%)
  blocking collectives  81.2 us (25%)
  local copies, waits for them, and re-layouts  29.1 us (9%)
  matrix products  15 us (5%)
  between operations  13.7 us (4%)
  other arithmetic  9.21 us (3%)
  starting transfers between devices  4.37 us (1%)
    psum x1, waiting for transfers between devices, broadcast(): return lax.psum(block, axis)  100 us
    psum x1, waiting for transfers between devices, shards(): lax.psum((local_total * shrink, rescale(local_acc, shrink)), 'seq')  74.6 us
    psum x1, blocking collectives, shards(): lax.psum((local_total * shrink, rescale(local_acc, shrink)), 'seq')  40.7 us
    pmax x1, blocking collectives, shards(): full_top = lax.pmax(local_top, 'seq')  40.5 us
  transfers between devices with their start and end apart: 4, of which 2 were waited for; matrix products, arithmetic and copies ran while one was open for 11% of the time, Pallas kernels for 0%

commit v1 on v0

v1 whole, which is shorter than its diff:
```python
import functools
import math

import jax
import jax.numpy as jnp
from jax import lax
from jax.experimental import pallas as pl
from jax.experimental.pallas import tpu as pltpu
from jax.sharding import PartitionSpec as P

H = 12
BLOCK = 64
NG = 128
GROUP = 8
PIECE = NG // GROUP
LANES = 128
MESH = pl.DeviceIdType.MESH
BF16 = jnp.bfloat16
F32 = jnp.float32


def dot_t(a, b):
    return lax.dot_general(a, b, (((1,), (1,)), ((), ())), preferred_element_type=F32)


def kernel(
    n, tok_in, wq_in, wk_in, wv_in, wo_in, gain_ref, bias_ref, out_ref,
    tok, wq, wk, wv, wo, q, k, v, qg, mask, pacc, pst, racc, rst, cacc, cst, zacc, zst,
    piece, gout, att,
    loc, halo_s, halo_r, s1s, s1r, s2s, s2r, s3s, s3r, r1s, r1r, r2s, r2r, r3s, r3r,
):
    rows, width = tok_in.shape
    chunks = rows // NG
    pairs = width // LANES
    groups = n // GROUP
    scale = 1.0 / math.sqrt(width // H)
    own = BLOCK
    right_at = BLOCK + rows
    glob = rows + 2 * BLOCK
    me = lax.axis_index("seq")
    g = me // GROUP
    j = me % GROUP
    base = g * GROUP

    def remote(src, dst, ss, rs, dev):
        return pltpu.make_async_remote_copy(
            src_ref=src, dst_ref=dst, send_sem=ss, recv_sem=rs, device_id=(dev,), device_id_type=MESH
        )

    local = [
        pltpu.make_async_copy(tok_in, tok.at[pl.ds(own, rows)], loc.at[0]),
        pltpu.make_async_copy(wq_in, wq, loc.at[1]),
        pltpu.make_async_copy(wk_in, wk, loc.at[2]),
        pltpu.make_async_copy(wv_in, wv, loc.at[3]),
        pltpu.make_async_copy(wo_in, wo, loc.at[4]),
    ]
    for copy in local:
        copy.start()

    barrier = pltpu.get_barrier_semaphore()

    def greet(dev):
        pl.semaphore_signal(barrier, inc=1, device_id=(dev,), device_id_type=MESH)

    for d in range(1, GROUP):
        greet(base + (j + d) % GROUP)

    @pl.when(g == 0)
    def _():
        for other in range(1, groups):
            greet(other * GROUP + j)

    @pl.when(g > 0)
    def _():
        greet(j)

    has_left = me > 0
    has_right = me < n - 1
    cross_left = (j == 0) & (g > 0)
    cross_right = (j == GROUP - 1) & (g < groups - 1)

    @pl.when(cross_left)
    def _():
        greet(me - 1)

    @pl.when(cross_right)
    def _():
        greet(me + 1)

    peers = GROUP - 1 + jnp.where(g == 0, groups - 1, 1) + jnp.where(cross_left, 1, 0) + jnp.where(cross_right, 1, 0)
    pl.semaphore_wait(barrier, peers)

    def glob_piece(index):
        return tok.at[pl.ds(pl.multiple_of(glob + index * PIECE, PIECE), PIECE)]

    def scatter(d):
        return remote(tok_in.at[pl.ds(d * PIECE, PIECE)], glob_piece(d), s1s.at[d], s1r.at[0], d)

    def climb(other):
        return remote(glob_piece(j), glob_piece(j), s2s.at[other], s2r.at[0], other * GROUP + j)

    def gather(d):
        t = (j + d) % GROUP
        return remote(glob_piece(j), glob_piece(j), s3s.at[d], s3r.at[d], base + t)

    keep = pltpu.make_async_copy(tok_in.at[pl.ds(0, NG)], tok.at[pl.ds(glob, NG)], loc.at[5])

    @pl.when(me == 0)
    def _():
        for d in range(1, GROUP):
            scatter(d).start()
        keep.start()

    to_left = remote(tok_in.at[pl.ds(0, BLOCK)], tok.at[pl.ds(right_at, BLOCK)], halo_s.at[0], halo_r.at[0], me - 1)
    to_right = remote(
        tok_in.at[pl.ds(rows - BLOCK, BLOCK)], tok.at[pl.ds(0, BLOCK)], halo_s.at[1], halo_r.at[1], me + 1
    )

    @pl.when(has_left)
    def _():
        to_left.start()

    @pl.when(has_right)
    def _():
        to_right.start()

    @pl.when(me == 0)
    def _():
        tok[0:BLOCK] = jnp.zeros((BLOCK, width), BF16)

    @pl.when(me == n - 1)
    def _():
        tok[right_at : right_at + BLOCK] = jnp.zeros((BLOCK, width), BF16)

    tile = 2 * LANES if width % (2 * LANES) == 0 else LANES

    def project(start, count, w, dst):
        @pl.loop(0, width // tile)
        def _(t):
            cols = pl.ds(pl.multiple_of(t * tile, tile), tile)
            dst[start : start + count, cols] = jnp.dot(
                tok[start : start + count], w[:, cols], preferred_element_type=F32
            ).astype(BF16)

    def project_query(start, count, dst):
        first_half = lax.broadcasted_iota(jnp.int32, (NG, tile), 1) % LANES < BLOCK

        @pl.loop(0, width // tile)
        def _(t):
            cols = pl.ds(pl.multiple_of(t * tile, tile), tile)
            res = jnp.dot(tok[start : start + count], wq[:, cols], preferred_element_type=F32) * scale
            for c in range(count // NG):
                part = res[c * NG : (c + 1) * NG]
                dst[2 * c * NG : (2 * c + 1) * NG, cols] = jnp.where(first_half, part, 0.0).astype(BF16)
                dst[(2 * c + 1) * NG : (2 * c + 2) * NG, cols] = jnp.where(first_half, 0.0, part).astype(BF16)

    local[0].wait()
    local[1].wait()
    project_query(own, rows, q)

    def gather_sends():
        for d in range(1, GROUP):
            @pl.when((g > 0) | ((j + d) % GROUP != 0))
            def _():
                gather(d).start()

    @pl.when(g == 0)
    def _():
        @pl.when(j > 0)
        def _():
            remote(glob_piece(j), glob_piece(j), s1s.at[0], s1r.at[0], 0).wait_recv()

        @pl.when(j == 0)
        def _():
            keep.wait()

        for other in range(1, groups):
            climb(other).start()
        gather_sends()

    local[2].wait()
    project(own, rows, wk, k)

    @pl.when(g > 0)
    def _():
        remote(glob_piece(j), glob_piece(j), s2s.at[0], s2r.at[0], j).wait_recv()
        gather_sends()

    local[3].wait()
    project(own, rows, wv, v)

    shape = (2 * NG, NG + 2 * BLOCK)
    row_block = lax.broadcasted_iota(jnp.int32, shape, 0) % NG // BLOCK
    key_id = lax.broadcasted_iota(jnp.int32, shape, 1)
    apart = key_id // BLOCK - row_block
    for c in range(chunks):
        place = me * rows + (c * NG - BLOCK) + key_id
        ok = (apart >= 0) & (apart <= 2) & (place >= NG) & (place < n * rows)
        mask[c] = jnp.where(ok, 0.0, -jnp.inf).astype(F32)

    @pl.when(me > 0)
    def _():
        for d in range(1, GROUP):
            t = (j + GROUP - d) % GROUP
            remote(glob_piece(t), glob_piece(t), s3s.at[d], s3r.at[d], base + t).wait_recv()

    project_query(glob, NG, qg)

    lane = lax.broadcasted_iota(jnp.int32, (NG, LANES), 1)
    low = lane < BLOCK
    pst[...] = jnp.zeros((NG, LANES), F32)

    @pl.loop(0, pairs)
    def _(p):
        cols = pl.ds(pl.multiple_of(p * LANES, LANES), LANES)
        s = dot_t(qg[:, cols], k[own : own + rows, cols])
        top = jnp.max(s, axis=-1, keepdims=True)
        e = jnp.exp(s - top)
        total = jnp.sum(e, axis=-1, keepdims=True)
        o = jnp.dot(e.astype(BF16), v[own : own + rows, cols], preferred_element_type=F32)
        pacc[:, cols] = jnp.where(low, o[:NG], o[NG:]).astype(BF16)
        st = pst[...]
        st = jnp.where(lane == 2 * p, top[:NG], st)
        st = jnp.where(lane == 2 * p + 1, top[NG:], st)
        st = jnp.where(lane == BLOCK + 2 * p, total[:NG], st)
        st = jnp.where(lane == BLOCK + 2 * p + 1, total[NG:], st)
        pst[...] = st

    def part(index):
        return pl.ds(pl.multiple_of(index * PIECE, PIECE), PIECE)

    def spread(d):
        t = (j + d) % GROUP
        return (
            remote(pacc.at[part(t)], racc.at[d], r1s.at[0, d], r1r.at[0, d], base + t),
            remote(pst.at[part(t)], rst.at[d], r1s.at[1, d], r1r.at[1, d], base + t),
        )

    for d in range(1, GROUP):
        for copy in spread(d):
            copy.start()
    racc[0] = pacc[part(j)]
    rst[0] = pst[part(j)]

    small_lane = lax.broadcasted_iota(jnp.int32, (PIECE, LANES), 1)
    small_low = small_lane < BLOCK

    def per_head(x, p, offset):
        return jnp.where(
            small_low, x[:, offset + 2 * p : offset + 2 * p + 1], x[:, offset + 2 * p + 1 : offset + 2 * p + 2]
        )

    def combine(count, accs, sts):
        st = [sts[d] for d in range(count)]
        top = functools.reduce(jnp.maximum, st)
        factors = [jnp.exp(s - top) for s in st]
        total = sum(pltpu.roll(f, BLOCK, 1) * s for f, s in zip(factors, st))
        sums = []
        for p in range(pairs):
            cols = slice(p * LANES, (p + 1) * LANES)
            sums.append(sum(per_head(factors[d], p, 0) * accs[d, :, cols].astype(F32) for d in range(count)))
        return sums, jnp.where(small_low, top, total)

    def window(c, p):
        cols = pl.ds(pl.multiple_of(p * LANES, LANES), LANES)
        span = slice(c * NG, c * NG + NG + 2 * BLOCK)
        qs = q[2 * c * NG : 2 * (c + 1) * NG, cols]
        sw = dot_t(qs, k[span, cols]) + mask[c]
        sg = dot_t(qs, k[glob : glob + NG, cols])
        top = jnp.maximum(jnp.max(sw, axis=-1, keepdims=True), jnp.max(sg, axis=-1, keepdims=True))
        ew = jnp.exp(sw - top)
        eg = jnp.exp(sg - top)
        total = jnp.sum(ew, axis=-1, keepdims=True) + jnp.sum(eg, axis=-1, keepdims=True)
        o = jnp.dot(ew.astype(BF16), v[span, cols], preferred_element_type=F32)
        o = o + jnp.dot(eg.astype(BF16), v[glob : glob + NG, cols], preferred_element_type=F32)
        o = o / total
        att[c * NG : (c + 1) * NG, cols] = jnp.where(low, o[:NG], o[NG:]).astype(BF16)

    def windows(c, first, last):
        @pl.loop(first, last)
        def _(p):
            window(c, p)

    def finish(c):
        at = slice(c * NG, (c + 1) * NG)
        proj = jnp.dot(att[at], wo[...], preferred_element_type=F32)
        summed = tok[own + c * NG : own + (c + 1) * NG].astype(F32) + proj
        center = summed - jnp.mean(summed, axis=-1, keepdims=True)
        spread_ = jnp.mean(center * center, axis=-1, keepdims=True)
        out_ref[at] = (center * lax.rsqrt(spread_ + 1e-05) * gain_ref[...] + bias_ref[...]).astype(BF16)

    @pl.when(has_left)
    def _():
        to_right.wait_recv()

    @pl.when(has_right)
    def _():
        to_left.wait_recv()

    for w, dst in ((wk, k), (wv, v)):
        project(0, BLOCK, w, dst)
        project(right_at, BLOCK + NG, w, dst)

    half = pairs // 2
    last = chunks - 1
    windows(last, 0, half)

    for d in range(1, GROUP):
        for copy in spread(d):
            copy.wait_recv()
    sums, st = combine(GROUP, racc, rst)

    @pl.when(g == 0)
    def _():
        for p in range(pairs):
            zacc[0, :, p * LANES : (p + 1) * LANES] = sums[p].astype(BF16)
        zst[0] = st

    def raise_up():
        return (
            remote(cacc, zacc.at[g], r2s.at[0], r2r.at[0, g], j),
            remote(cst, zst.at[g], r2s.at[1], r2r.at[1, g], j),
        )

    @pl.when(g > 0)
    def _():
        for p in range(pairs):
            cacc[:, p * LANES : (p + 1) * LANES] = sums[p].astype(BF16)
        cst[...] = st
        for copy in raise_up():
            copy.start()

    windows(last, half, pairs)
    for c in range(last):
        windows(c, 0, half)

    deliver = remote(piece, gout.at[part(j)], r3s.at[0], r3r.at[j], 0)

    @pl.when(g == 0)
    def _():
        for other in range(1, groups):
            remote(cacc, zacc.at[other], r2s.at[0], r2r.at[0, other], other * GROUP + j).wait_recv()
            remote(cst, zst.at[other], r2s.at[1], r2r.at[1, other], other * GROUP + j).wait_recv()
        full, full_st = combine(groups, zacc, zst)
        for p in range(pairs):
            piece[:, p * LANES : (p + 1) * LANES] = (full[p] / per_head(full_st, p, BLOCK)).astype(BF16)

        @pl.when(j > 0)
        def _():
            deliver.start()

        @pl.when(j == 0)
        def _():
            gout[0:PIECE] = piece[...]

    for c in range(last):
        windows(c, half, pairs)
    local[4].wait()
    for c in range(1, chunks):
        finish(c)

    @pl.when(me == 0)
    def _():
        for d in range(1, GROUP):
            remote(piece, gout.at[pl.ds(d * PIECE, PIECE)], r3s.at[0], r3r.at[d], d).wait_recv()
        att[0:NG] = gout[...]

    finish(0)

    @pl.when(has_left)
    def _():
        to_left.wait_send()

    @pl.when(has_right)
    def _():
        to_right.wait_send()

    @pl.when(me == 0)
    def _():
        for d in range(1, GROUP):
            scatter(d).wait_send()

    @pl.when(g == 0)
    def _():
        for other in range(1, groups):
            climb(other).wait_send()

        @pl.when(j > 0)
        def _():
            deliver.wait_send()

    @pl.when(g > 0)
    def _():
        for copy in raise_up():
            copy.wait_send()

    for d in range(1, GROUP):
        @pl.when((g > 0) | ((j + d) % GROUP != 0))
        def _():
            gather(d).wait_send()

        for copy in spread(d):
            copy.wait_send()


def shards(n, tokens, w_query, w_key, w_value, w_out, ln_gain, ln_bias):
    rows, width = tokens.shape
    groups = n // GROUP
    ext = rows + 2 * BLOCK + NG
    dma = pltpu.SemaphoreType.DMA
    weight = pltpu.VMEM((width, width), BF16)
    scratch = [
        pltpu.VMEM((ext, width), BF16),
        weight, weight, weight, weight,
        pltpu.VMEM((2 * rows, width), BF16),
        pltpu.VMEM((ext, width), BF16),
        pltpu.VMEM((ext, width), BF16),
        pltpu.VMEM((2 * NG, width), BF16),
        pltpu.VMEM((rows // NG, 2 * NG, NG + 2 * BLOCK), F32),
        pltpu.VMEM((NG, width), BF16),
        pltpu.VMEM((NG, LANES), F32),
        pltpu.VMEM((GROUP, PIECE, width), BF16),
        pltpu.VMEM((GROUP, PIECE, LANES), F32),
        pltpu.VMEM((PIECE, width), BF16),
        pltpu.VMEM((PIECE, LANES), F32),
        pltpu.VMEM((groups, PIECE, width), BF16),
        pltpu.VMEM((groups, PIECE, LANES), F32),
        pltpu.VMEM((PIECE, width), BF16),
        pltpu.VMEM((NG, width), BF16),
        pltpu.VMEM((rows, width), BF16),
        dma((6,)), dma((2,)), dma((2,)),
        dma((GROUP,)), dma((1,)),
        dma((groups,)), dma((1,)),
        dma((GROUP,)), dma((GROUP,)),
        dma((2, GROUP)), dma((2, GROUP)),
        dma((2,)), dma((2, groups)),
        dma((1,)), dma((GROUP,)),
    ]
    anywhere = pl.BlockSpec(memory_space=pl.ANY)
    vmem = pl.BlockSpec(memory_space=pltpu.VMEM)
    return pl.pallas_call(
        functools.partial(kernel, n),
        out_shape=jax.ShapeDtypeStruct((rows, width), BF16),
        in_specs=[anywhere] * 5 + [vmem] * 2,
        out_specs=vmem,
        scratch_shapes=scratch,
        compiler_params=pltpu.CompilerParams(
            collective_id=0, has_side_effects=True, vmem_limit_bytes=40 * 1024 * 1024
        ),
    )(tokens, w_query, w_key, w_value, w_out, ln_gain.reshape(1, width), ln_bias.reshape(1, width))


def solution(mesh):
    n = mesh.shape["seq"]
    in_specs = (P("seq", None), P(), P(), P(), P(), P(), P())
    return jax.shard_map(
        functools.partial(shards, n), mesh=mesh, in_specs=in_specs, out_specs=P("seq", None), check_vma=False
    )
```

time: 328 us -> 45.7 us (0.14)
  waiting for transfers between devices: 175 us -> 0 us
  blocking collectives: 81.2 us -> 0 us
  Pallas kernels: 0 us -> 37.1 us
  local copies, waits for them, and re-layouts: 29.1 us -> 8.2 us
  matrix products: 15 us -> 0 us
  between operations: 13.7 us -> 0.02 us
  other arithmetic: 9.21 us -> 0 us
  starting transfers between devices: 4.37 us -> 0 us
    psum x2 -> x0, waiting for transfers between devices: 175 us -> none  [the longest x1 100 us: broadcast(): return lax.psum(block, axis)]
    psum x1 -> x0, blocking collectives: 40.7 us -> none  [shards(): lax.psum((local_total * shrink, rescale(local_acc, shrink)), 'seq')]
    pmax x1 -> x0, blocking collectives: 40.5 us -> none  [shards(): full_top = lax.pmax(local_top, 'seq')]
    pallas_call x0 -> x1, Pallas kernels: none -> 37.1 us  [shards(): pl.pallas_call(functools.partial(kernel, n), out_shape=jax.ShapeDtypeStru...]
    slice x16 -> x0, local copies, waits for them, and re-layouts: 21.9 us -> none  [the longest x2 4.1 us: shards(): value_grid[1:-1]]
    dot_general x8 -> x0, matrix products: 15 us -> none  [the longest x3 4.37 us: project(): jnp.dot(inputs, weight, preferred_element_type=jnp.float32)]
    unnamed x24 -> x11, local copies, waits for them, and re-layouts: 0.79 us -> 6.82 us
    ppermute x2 -> x0, starting transfers between devices: 4.33 us -> none  [the longest x1 3.05 us: with_halo(): lax.ppermute(tail, axis, [(i, (i + 1) % count) for i in range(ends)])]
  transfers between devices with their start and end apart: 4 -> 0, of which waited for: 2 -> 0; matrix products, arithmetic and copies ran while one was open for 11% -> 0% of each run, Pallas kernels for 0% -> 0%
where the time goes in v1:
time: 45.7 us; the launch traced here: 45.3 us
  Pallas kernels  37.1 us (81%)
  local copies, waits for them, and re-layouts  8.2 us (18%)
    pallas_call x1, Pallas kernels, shards(): pl.pallas_call(functools.partial(kernel, n), out_shape=jax.ShapeDtypeStru...  37.1 us
    unnamed x11, local copies, waits for them, and re-layouts  6.82 us

profile of v1, /device:TPU:0, one launch (start us, length us, event | category | flops | bytes accessed | tf_op | source)
XLA Modules:
  0.0 45.3 jit_solution(10980886866683249526)
XLA Ops:
  0.0 0.7 %reshape.6.gain_ref = f32[1,768]{1,0:T(1,128)S(1)} reshape(f32[768]{0:T(1024)} %param.12) | data formatting | bytes 6144 | tf_op jit(solution)/shard_map/reshape | solution.py:450
  0.7 0.7 %reshape.7.bias_ref = f32[1,768]{1,0:T(1,128)S(1)} reshape(f32[768]{0:T(1024)} %param.13) | data formatting | bytes 6144 | tf_op jit(solution)/shard_map/reshape | solution.py:450
  1.4 0.0 copy-start
  1.4 1.3 %copy-done = bf16[768,768]{1,0:T(8,128)(2,1)S(1)} copy-done((bf16[768,768]{1,0:T(8,128)(2,1)S(1)}, bf16[768,768]{1,0:T(8,128)(2,1)}, u32[]{:S(2)}) %copy-start) | copy-done | bytes 1179672
  2.7 0.0 copy-start.1
  2.7 1.3 %copy-done.1 = bf16[768,768]{1,0:T(8,128)(2,1)S(1)} copy-done((bf16[768,768]{1,0:T(8,128)(2,1)S(1)}, bf16[768,768]{1,0:T(8,128)(2,1)}, u32[]{:S(2)}) %copy-start.1) | copy-done | bytes 1179672
  3.9 0.0 copy-start.2
  3.9 1.3 %copy-done.2 = bf16[768,768]{1,0:T(8,128)(2,1)S(1)} copy-done((bf16[768,768]{1,0:T(8,128)(2,1)S(1)}, bf16[768,768]{1,0:T(8,128)(2,1)}, u32[]{:S(2)}) %copy-start.2) | copy-done | bytes 1179672
  5.2 0.0 copy-start.3
  5.2 1.3 %copy-done.3 = bf16[768,768]{1,0:T(8,128)(2,1)S(1)} copy-done((bf16[768,768]{1,0:T(8,128)(2,1)S(1)}, bf16[768,768]{1,0:T(8,128)(2,1)}, u32[]{:S(2)}) %copy-start.3) | copy-done | bytes 1179672
  6.5 0.0 copy-start.4
  6.5 1.0 %copy-done.4 = bf16[256,768]{1,0:T(8,128)(2,1)S(1)} copy-done((bf16[256,768]{1,0:T(8,128)(2,1)S(1)}, bf16[256,768]{1,0:T(8,128)(2,1)}, u32[]{:S(2)}) %copy-start.4) | copy-done | bytes 393240
  7.5 37.1 %shard_map.73 = bf16[256,768]{1,0:T(8,128)(2,1)S(1)} custom-call(bf16[256,768]{1,0:T(8,128)(2,1)S(1)} %copy-done.4, bf16[768,768]{1,0:T(8,128)(2,1)S(1)} %copy-done, bf16[768,768]{1,0:T(8,128)(2,1)S(1)} %copy-done.1, bf16[768,768]{1,0:T(8,128)(2,1)S(1)} %copy-done.2, bf16[768,768]{1,0:T(8,128)(2,1)S(1)} %copy-done.3, f32[1,768]{1,0:T(1,128)S(1)} %reshape.6.gain_ref, ...), custom_call_target="tpu_custom_call" | custom-call | tf_op jit(solution)/shard_map/pallas_call | solution.py:441
  44.6 0.7 %copy.9 = bf16[256,768]{1,0:T(8,128)(2,1)} copy(bf16[256,768]{1,0:T(8,128)(2,1)S(1)} %shard_map.73) | data formatting | bytes 786432
Async XLA Ops:
  1.4 1.3 %copy-start = (bf16[768,768]{1,0:T(8,128)(2,1)S(1)}, bf16[768,768]{1,0:T(8,128)(2,1)}, u32[]{:S(2)}) copy-start(bf16[768,768]{1,0:T(8,128)(2,1)} %wq_in.1) | copy-start | bytes 3538948
  2.7 1.3 %copy-start.1 = (bf16[768,768]{1,0:T(8,128)(2,1)S(1)}, bf16[768,768]{1,0:T(8,128)(2,1)}, u32[]{:S(2)}) copy-start(bf16[768,768]{1,0:T(8,128)(2,1)} %wk_in.1) | copy-start | bytes 3538948
  3.9 1.3 %copy-start.2 = (bf16[768,768]{1,0:T(8,128)(2,1)S(1)}, bf16[768,768]{1,0:T(8,128)(2,1)}, u32[]{:S(2)}) copy-start(bf16[768,768]{1,0:T(8,128)(2,1)} %wv_in.1) | copy-start | bytes 3538948
  5.2 1.3 %copy-start.3 = (bf16[768,768]{1,0:T(8,128)(2,1)S(1)}, bf16[768,768]{1,0:T(8,128)(2,1)}, u32[]{:S(2)}) copy-start(bf16[768,768]{1,0:T(8,128)(2,1)} %wo_in.1) | copy-start | bytes 3538948
  6.5 1.0 %copy-start.4 = (bf16[256,768]{1,0:T(8,128)(2,1)S(1)}, bf16[256,768]{1,0:T(8,128)(2,1)}, u32[]{:S(2)}) copy-start(bf16[256,768]{1,0:T(8,128)(2,1)} %tok_in.1) | copy-start | bytes 1179652

commit v2 on v1

--- a/solution.py
+++ b/solution.py
@@ -24,8 +24,8 @@
 
 
 def kernel(
-    n, tok_in, wq_in, wk_in, wv_in, wo_in, gain_ref, bias_ref, out_ref,
-    tok, wq, wk, wv, wo, q, k, v, qg, mask, pacc, pst, racc, rst, cacc, cst, zacc, zst,
+    n, tok_in, wq_in, wk_in, wv_in, wo_in, gain_in, bias_in, out_ref,
+    tok, wq, wk, wv, wo, gain_ref, bias_ref, q, k, v, qg, mask, pacc, pst, racc, cacc, zacc,
     piece, gout, att,
     loc, halo_s, halo_r, s1s, s1r, s2s, s2r, s3s, s3r, r1s, r1r, r2s, r2r, r3s, r3r,
 ):
@@ -53,8 +53,10 @@
         pltpu.make_async_copy(wk_in, wk, loc.at[2]),
         pltpu.make_async_copy(wv_in, wv, loc.at[3]),
         pltpu.make_async_copy(wo_in, wo, loc.at[4]),
+        pltpu.make_async_copy(gain_in, gain_ref, loc.at[6]),
+        pltpu.make_async_copy(bias_in, bias_ref, loc.at[7]),
     ]
-    for copy in local:
+    for copy in local[:2]:
         copy.start()
 
     barrier = pltpu.get_barrier_semaphore()
@@ -123,6 +125,9 @@
     @pl.when(has_right)
     def _():
         to_right.start()
+
+    for copy in local[2:]:
+        copy.start()
 
     @pl.when(me == 0)
     def _():
@@ -229,18 +234,28 @@
     def part(index):
         return pl.ds(pl.multiple_of(index * PIECE, PIECE), PIECE)
 
+    def encode(x):
+        hi = x.astype(BF16)
+        rest = x - hi.astype(F32)
+        mid = rest.astype(BF16)
+        lo = (rest - mid.astype(F32)).astype(BF16)
+        return (
+            hi.astype(F32) + pltpu.roll(mid.astype(F32), 16, 1) + pltpu.roll(lo.astype(F32), 32, 1)
+        ).astype(BF16)
+
+    def decode(x):
+        x = x.astype(F32)
+        return x + pltpu.roll(x, LANES - 16, 1) + pltpu.roll(x, LANES - 32, 1)
+
+    pacc[:, width:] = encode(pst[...])
+
     def spread(d):
         t = (j + d) % GROUP
-        return (
-            remote(pacc.at[part(t)], racc.at[d], r1s.at[0, d], r1r.at[0, d], base + t),
-            remote(pst.at[part(t)], rst.at[d], r1s.at[1, d], r1r.at[1, d], base + t),
-        )
+        return remote(pacc.at[part(t)], racc.at[d], r1s.at[d], r1r.at[d], base + t)
 
     for d in range(1, GROUP):
-        for copy in spread(d):
-            copy.start()
+        spread(d).start()
     racc[0] = pacc[part(j)]
-    rst[0] = pst[part(j)]
 
     small_lane = lax.broadcasted_iota(jnp.int32, (PIECE, LANES), 1)
     small_low = small_lane < BLOCK
@@ -250,8 +265,8 @@
             small_low, x[:, offset + 2 * p : offset + 2 * p + 1], x[:, offset + 2 * p + 1 : offset + 2 * p + 2]
         )
 
-    def combine(count, accs, sts):
-        st = [sts[d] for d in range(count)]
+    def combine(count, accs):
+        st = [decode(accs[d, :, width:]) for d in range(count)]
         top = functools.reduce(jnp.maximum, st)
         factors = [jnp.exp(s - top) for s in st]
         total = sum(pltpu.roll(f, BLOCK, 1) * s for f, s in zip(factors, st))
@@ -259,7 +274,8 @@
         for p in range(pairs):
             cols = slice(p * LANES, (p + 1) * LANES)
             sums.append(sum(per_head(factors[d], p, 0) * accs[d, :, cols].astype(F32) for d in range(count)))
-        return sums, jnp.where(small_low, top, total)
+        st = jnp.where(small_low, top, total)
+        return sums, jnp.where(small_lane % BLOCK < H, st, 0.0)
 
     def window(c, p):
         cols = pl.ds(pl.multiple_of(p * LANES, LANES), LANES)
@@ -287,7 +303,7 @@
         summed = tok[own + c * NG : own + (c + 1) * NG].astype(F32) + proj
         center = summed - jnp.mean(summed, axis=-1, keepdims=True)
         spread_ = jnp.mean(center * center, axis=-1, keepdims=True)
-        out_ref[at] = (center * lax.rsqrt(spread_ + 1e-05) * gain_ref[...] + bias_ref[...]).astype(BF16)
+        out_ref[at] = (center * lax.rsqrt(spread_ + 1e-05) * gain_ref[...][None] + bias_ref[...][None]).astype(BF16)
 
     @pl.when(has_left)
     def _():
@@ -306,29 +322,24 @@
     windows(last, 0, half)
 
     for d in range(1, GROUP):
-        for copy in spread(d):
-            copy.wait_recv()
-    sums, st = combine(GROUP, racc, rst)
+        spread(d).wait_recv()
+    sums, st = combine(GROUP, racc)
+
+    def pack(dst, slot):
+        for p in range(pairs):
+            dst[slot, :, p * LANES : (p + 1) * LANES] = sums[p].astype(BF16)
+        dst[slot, :, width:] = encode(st)
+
+    raise_up = remote(cacc.at[0], zacc.at[g], r2s.at[0], r2r.at[g], j)
 
     @pl.when(g == 0)
     def _():
-        for p in range(pairs):
-            zacc[0, :, p * LANES : (p + 1) * LANES] = sums[p].astype(BF16)
-        zst[0] = st
-
-    def raise_up():
-        return (
-            remote(cacc, zacc.at[g], r2s.at[0], r2r.at[0, g], j),
-            remote(cst, zst.at[g], r2s.at[1], r2r.at[1, g], j),
-        )
+        pack(zacc, 0)
 
     @pl.when(g > 0)
     def _():
-        for p in range(pairs):
-            cacc[:, p * LANES : (p + 1) * LANES] = sums[p].astype(BF16)
-        cst[...] = st
-        for copy in raise_up():
-            copy.start()
+        pack(cacc, 0)
+        raise_up.start()
 
     windows(last, half, pairs)
     for c in range(last):
@@ -339,9 +350,8 @@
     @pl.when(g == 0)
     def _():
         for other in range(1, groups):
-            remote(cacc, zacc.at[other], r2s.at[0], r2r.at[0, other], other * GROUP + j).wait_recv()
-            remote(cst, zst.at[other], r2s.at[1], r2r.at[1, other], other * GROUP + j).wait_recv()
-        full, full_st = combine(groups, zacc, zst)
+            remote(cacc.at[0], zacc.at[other], r2s.at[0], r2r.at[other], other * GROUP + j).wait_recv()
+        full, full_st = combine(groups, zacc)
         for p in range(pairs):
             piece[:, p * LANES : (p + 1) * LANES] = (full[p] / per_head(full_st, p, BLOCK)).astype(BF16)
 
@@ -355,7 +365,8 @@
 
     for c in range(last):
         windows(c, half, pairs)
-    local[4].wait()
+    for copy in local[4:]:
+        copy.wait()
     for c in range(1, chunks):
         finish(c)
 
@@ -391,16 +402,14 @@
 
     @pl.when(g > 0)
     def _():
-        for copy in raise_up():
-            copy.wait_send()
+        raise_up.wait_send()
 
     for d in range(1, GROUP):
         @pl.when((g > 0) | ((j + d) % GROUP != 0))
         def _():
             gather(d).wait_send()
 
-        for copy in spread(d):
-            copy.wait_send()
+        spread(d).wait_send()
 
 
 def shards(n, tokens, w_query, w_key, w_value, w_out, ln_gain, ln_bias):
@@ -412,28 +421,27 @@
     scratch = [
         pltpu.VMEM((ext, width), BF16),
         weight, weight, weight, weight,
+        pltpu.VMEM((width,), F32),
+        pltpu.VMEM((width,), F32),
         pltpu.VMEM((2 * rows, width), BF16),
         pltpu.VMEM((ext, width), BF16),
         pltpu.VMEM((ext, width), BF16),
         pltpu.VMEM((2 * NG, width), BF16),
         pltpu.VMEM((rows // NG, 2 * NG, NG + 2 * BLOCK), F32),
-        pltpu.VMEM((NG, width), BF16),
+        pltpu.VMEM((NG, width + LANES), BF16),
         pltpu.VMEM((NG, LANES), F32),
-        pltpu.VMEM((GROUP, PIECE, width), BF16),
-        pltpu.VMEM((GROUP, PIECE, LANES), F32),
-        pltpu.VMEM((PIECE, width), BF16),
-        pltpu.VMEM((PIECE, LANES), F32),
-        pltpu.VMEM((groups, PIECE, width), BF16),
-        pltpu.VMEM((groups, PIECE, LANES), F32),
+        pltpu.VMEM((GROUP, PIECE, width + LANES), BF16),
+        pltpu.VMEM((1, PIECE, width + LANES), BF16),
+        pltpu.VMEM((groups, PIECE, width + LANES), BF16),
         pltpu.VMEM((PIECE, width), BF16),
         pltpu.VMEM((NG, width), BF16),
         pltpu.VMEM((rows, width), BF16),
-        dma((6,)), dma((2,)), dma((2,)),
+        dma((8,)), dma((2,)), dma((2,)),
         dma((GROUP,)), dma((1,)),
         dma((groups,)), dma((1,)),
         dma((GROUP,)), dma((GROUP,)),
-        dma((2, GROUP)), dma((2, GROUP)),
-        dma((2,)), dma((2, groups)),
+        dma((GROUP,)), dma((GROUP,)),
+        dma((1,)), dma((groups,)),
         dma((1,)), dma((GROUP,)),
     ]
     anywhere = pl.BlockSpec(memory_space=pl.ANY)
@@ -441,13 +449,13 @@
     return pl.pallas_call(
         functools.partial(kernel, n),
         out_shape=jax.ShapeDtypeStruct((rows, width), BF16),
-        in_specs=[anywhere] * 5 + [vmem] * 2,
+        in_specs=[anywhere] * 7,
         out_specs=vmem,
         scratch_shapes=scratch,
         compiler_params=pltpu.CompilerParams(
-            collective_id=0, has_side_effects=True, vmem_limit_bytes=40 * 1024 * 1024
+            collective_id=0, has_side_effects=True, vmem_limit_bytes=60 * 1024 * 1024
         ),
-    )(tokens, w_query, w_key, w_value, w_out, ln_gain.reshape(1, width), ln_bias.reshape(1, width))
+    )(tokens, w_query, w_key, w_value, w_out, ln_gain, ln_bias)
 
 
 def solution(mesh):

time: 45.7 us -> 38.5 us (0.84)
  local copies, waits for them, and re-layouts: 8.2 us -> 1.77 us
  Pallas kernels: 37.1 us -> 36.6 us
    unnamed x11 -> x1, local copies, waits for them, and re-layouts: 6.82 us -> 1.77 us
    reshape x2 -> x0, local copies, waits for them, and re-layouts: 1.38 us -> none  [the longest x1 0.69 us: shards(): ln_bias.reshape(1, width)]
    pallas_call x1, Pallas kernels: 37.1 us -> 36.6 us  [shards(): pl.pallas_call(functools.partial(kernel, n), out_shape=jax.ShapeDtypeStru...]
where the time goes in v2:
time: 38.5 us; the launch traced here: 38.4 us
  Pallas kernels  36.6 us (95%)
  local copies, waits for them, and re-layouts  1.77 us (5%)
    pallas_call x1, Pallas kernels, shards(): pl.pallas_call(functools.partial(kernel, n), out_shape=jax.ShapeDtypeStru...  36.6 us
    unnamed x1, local copies, waits for them, and re-layouts  1.77 us

profile of v2, /device:TPU:0, one launch (start us, length us, event | category | flops | bytes accessed | tf_op | source)
XLA Modules:
  0.0 38.4 jit_solution(4320707574985625994)
XLA Ops:
  0.0 36.6 %shard_map.73 = bf16[256,768]{1,0:T(8,128)(2,1)} custom-call(bf16[256,768]{1,0:T(8,128)(2,1)} %tok_in.1, bf16[768,768]{1,0:T(8,128)(2,1)} %wq_in.1, bf16[768,768]{1,0:T(8,128)(2,1)} %wk_in.1, bf16[768,768]{1,0:T(8,128)(2,1)} %wv_in.1, bf16[768,768]{1,0:T(8,128)(2,1)} %wo_in.1, f32[768]{0:T(1024)} %gain_in.1, f32[768]{0:T(1024)} %bias_in.1), custom_call_target="tpu_custom_call" | custom-call | tf_op jit(solution)/shard_map/pallas_call | solution.py:449
  36.6 1.8 %copy.9 = bf16[256,768]{1,0:T(8,128)(2,1)} copy(bf16[256,768]{1,0:T(8,128)(2,1)} %shard_map.73) | data formatting | bytes 786432

commit v3 on v2

--- a/solution.py
+++ b/solution.py
@@ -25,7 +25,7 @@
 
 def kernel(
     n, tok_in, wq_in, wk_in, wv_in, wo_in, gain_in, bias_in, out_ref,
-    tok, wq, wk, wv, wo, gain_ref, bias_ref, q, k, v, qg, mask, pacc, pst, racc, cacc, zacc,
+    tok, wq, wk, wv, wo, gain_ref, bias_ref, q, k, v, qg, mask, pacc, racc, cacc, zacc,
     piece, gout, att,
     loc, halo_s, halo_r, s1s, s1r, s2s, s2r, s3s, s3r, r1s, r1r, r2s, r2r, r3s, r3r,
 ):
@@ -203,6 +203,18 @@
         ok = (apart >= 0) & (apart <= 2) & (place >= NG) & (place < n * rows)
         mask[c] = jnp.where(ok, 0.0, -jnp.inf).astype(F32)
 
+    @pl.when(has_left)
+    def _():
+        to_right.wait_recv()
+
+    @pl.when(has_right)
+    def _():
+        to_left.wait_recv()
+
+    for w, dst in ((wk, k), (wv, v)):
+        project(0, BLOCK, w, dst)
+        project(right_at, BLOCK, w, dst)
+
     @pl.when(me > 0)
     def _():
         for d in range(1, GROUP):
@@ -213,27 +225,6 @@
 
     lane = lax.broadcasted_iota(jnp.int32, (NG, LANES), 1)
     low = lane < BLOCK
-    pst[...] = jnp.zeros((NG, LANES), F32)
-
-    @pl.loop(0, pairs)
-    def _(p):
-        cols = pl.ds(pl.multiple_of(p * LANES, LANES), LANES)
-        s = dot_t(qg[:, cols], k[own : own + rows, cols])
-        top = jnp.max(s, axis=-1, keepdims=True)
-        e = jnp.exp(s - top)
-        total = jnp.sum(e, axis=-1, keepdims=True)
-        o = jnp.dot(e.astype(BF16), v[own : own + rows, cols], preferred_element_type=F32)
-        pacc[:, cols] = jnp.where(low, o[:NG], o[NG:]).astype(BF16)
-        st = pst[...]
-        st = jnp.where(lane == 2 * p, top[:NG], st)
-        st = jnp.where(lane == 2 * p + 1, top[NG:], st)
-        st = jnp.where(lane == BLOCK + 2 * p, total[:NG], st)
-        st = jnp.where(lane == BLOCK + 2 * p + 1, total[NG:], st)
-        pst[...] = st
-
-    def part(index):
-        return pl.ds(pl.multiple_of(index * PIECE, PIECE), PIECE)
-
     def encode(x):
         hi = x.astype(BF16)
         rest = x - hi.astype(F32)
@@ -247,15 +238,34 @@
         x = x.astype(F32)
         return x + pltpu.roll(x, LANES - 16, 1) + pltpu.roll(x, LANES - 32, 1)
 
-    pacc[:, width:] = encode(pst[...])
-
-    def spread(d):
+    def part(index):
+        return pl.ds(pl.multiple_of(index * PIECE, PIECE), PIECE)
+
+    hp = pairs // 2
+    wide = hp * LANES
+
+    def spread(h, d):
         t = (j + d) % GROUP
-        return remote(pacc.at[part(t)], racc.at[d], r1s.at[d], r1r.at[d], base + t)
-
-    for d in range(1, GROUP):
-        spread(d).start()
-    racc[0] = pacc[part(j)]
+        return remote(pacc.at[h, part(t)], racc.at[h, d], r1s.at[h, d], r1r.at[h, d], base + t)
+
+    for h in range(2):
+        st = jnp.zeros((NG, LANES), F32)
+        for i in range(hp):
+            cols = slice((h * hp + i) * LANES, (h * hp + i + 1) * LANES)
+            s = dot_t(qg[:, cols], k[own : own + rows, cols])
+            top = jnp.max(s, axis=-1, keepdims=True)
+            e = jnp.exp(s - top)
+            total = jnp.sum(e, axis=-1, keepdims=True)
+            o = jnp.dot(e.astype(BF16), v[own : own + rows, cols], preferred_element_type=F32)
+            pacc[h, :, i * LANES : (i + 1) * LANES] = jnp.where(low, o[:NG], o[NG:]).astype(BF16)
+            st = jnp.where(lane == 2 * i, top[:NG], st)
+            st = jnp.where(lane == 2 * i + 1, top[NG:], st)
+            st = jnp.where(lane == BLOCK + 2 * i, total[:NG], st)
+            st = jnp.where(lane == BLOCK + 2 * i + 1, total[NG:], st)
+        pacc[h, :, wide:] = encode(st)
+        for d in range(1, GROUP):
+            spread(h, d).start()
+        racc[h, 0] = pacc[h, part(j)]
 
     small_lane = lax.broadcasted_iota(jnp.int32, (PIECE, LANES), 1)
     small_low = small_lane < BLOCK
@@ -265,17 +275,17 @@
             small_low, x[:, offset + 2 * p : offset + 2 * p + 1], x[:, offset + 2 * p + 1 : offset + 2 * p + 2]
         )
 
-    def combine(count, accs):
-        st = [decode(accs[d, :, width:]) for d in range(count)]
+    def combine(count, accs, h):
+        st = [decode(accs[h, d, :, wide:]) for d in range(count)]
         top = functools.reduce(jnp.maximum, st)
         factors = [jnp.exp(s - top) for s in st]
         total = sum(pltpu.roll(f, BLOCK, 1) * s for f, s in zip(factors, st))
         sums = []
-        for p in range(pairs):
+        for p in range(hp):
             cols = slice(p * LANES, (p + 1) * LANES)
-            sums.append(sum(per_head(factors[d], p, 0) * accs[d, :, cols].astype(F32) for d in range(count)))
+            sums.append(sum(per_head(factors[d], p, 0) * accs[h, d, :, cols].astype(F32) for d in range(count)))
         st = jnp.where(small_low, top, total)
-        return sums, jnp.where(small_lane % BLOCK < H, st, 0.0)
+        return sums, jnp.where(small_lane % BLOCK < 2 * hp, st, 0.0)
 
     def window(c, p):
         cols = pl.ds(pl.multiple_of(p * LANES, LANES), LANES)
@@ -293,9 +303,10 @@
         att[c * NG : (c + 1) * NG, cols] = jnp.where(low, o[:NG], o[NG:]).astype(BF16)
 
     def windows(c, first, last):
-        @pl.loop(first, last)
+        @pl.loop(first, last, step=2)
         def _(p):
             window(c, p)
+            window(c, p + 1)
 
     def finish(c):
         at = slice(c * NG, (c + 1) * NG)
@@ -305,66 +316,59 @@
         spread_ = jnp.mean(center * center, axis=-1, keepdims=True)
         out_ref[at] = (center * lax.rsqrt(spread_ + 1e-05) * gain_ref[...][None] + bias_ref[...][None]).astype(BF16)
 
-    @pl.when(has_left)
-    def _():
-        to_right.wait_recv()
-
-    @pl.when(has_right)
-    def _():
-        to_left.wait_recv()
-
     for w, dst in ((wk, k), (wv, v)):
-        project(0, BLOCK, w, dst)
-        project(right_at, BLOCK + NG, w, dst)
-
-    half = pairs // 2
+        project(glob, NG, w, dst)
+
     last = chunks - 1
-    windows(last, 0, half)
-
-    for d in range(1, GROUP):
-        spread(d).wait_recv()
-    sums, st = combine(GROUP, racc)
-
-    def pack(dst, slot):
-        for p in range(pairs):
-            dst[slot, :, p * LANES : (p + 1) * LANES] = sums[p].astype(BF16)
-        dst[slot, :, width:] = encode(st)
-
-    raise_up = remote(cacc.at[0], zacc.at[g], r2s.at[0], r2r.at[g], j)
+    early = min(4, pairs)
+    windows(last, 0, early)
+
+    def raise_up(h):
+        return remote(cacc.at[h], zacc.at[h, g], r2s.at[h], r2r.at[h, g], j)
+
+    for h in range(2):
+        for d in range(1, GROUP):
+            spread(h, d).wait_recv()
+        sums, st = combine(GROUP, racc, h)
+        sent = [x.astype(BF16) for x in sums] + [encode(st)]
+
+        @pl.when(g == 0)
+        def _():
+            for p in range(hp + 1):
+                zacc[h, 0, :, p * LANES : (p + 1) * LANES] = sent[p]
+
+        @pl.when(g > 0)
+        def _():
+            for p in range(hp + 1):
+                cacc[h, :, p * LANES : (p + 1) * LANES] = sent[p]
+            raise_up(h).start()
+
+    windows(last, early, pairs)
+    for c in range(last):
+        windows(c, 0, pairs)
+
+    def deliver(h):
+        return remote(piece.at[h], gout.at[h, part(j)], r3s.at[h], r3r.at[h, j], 0)
 
     @pl.when(g == 0)
     def _():
-        pack(zacc, 0)
-
-    @pl.when(g > 0)
-    def _():
-        pack(cacc, 0)
-        raise_up.start()
-
-    windows(last, half, pairs)
-    for c in range(last):
-        windows(c, 0, half)
-
-    deliver = remote(piece, gout.at[part(j)], r3s.at[0], r3r.at[j], 0)
-
-    @pl.when(g == 0)
-    def _():
-        for other in range(1, groups):
-            remote(cacc.at[0], zacc.at[other], r2s.at[0], r2r.at[other], other * GROUP + j).wait_recv()
-        full, full_st = combine(groups, zacc)
-        for p in range(pairs):
-            piece[:, p * LANES : (p + 1) * LANES] = (full[p] / per_head(full_st, p, BLOCK)).astype(BF16)
-
-        @pl.when(j > 0)
-        def _():
-            deliver.start()
-
-        @pl.when(j == 0)
-        def _():
-            gout[0:PIECE] = piece[...]
-
-    for c in range(last):
-        windows(c, half, pairs)
+        for h in range(2):
+            for other in range(1, groups):
+                remote(
+                    cacc.at[h], zacc.at[h, other], r2s.at[h], r2r.at[h, other], other * GROUP + j
+                ).wait_recv()
+            full, full_st = combine(groups, zacc, h)
+            for p in range(hp):
+                piece[h, :, p * LANES : (p + 1) * LANES] = (full[p] / per_head(full_st, p, BLOCK)).astype(BF16)
+
+            @pl.when(j > 0)
+            def _():
+                deliver(h).start()
+
+            @pl.when(j == 0)
+            def _():
+                gout[h, 0:PIECE] = piece[h]
+
     for copy in local[4:]:
         copy.wait()
     for c in range(1, chunks):
@@ -372,9 +376,12 @@
 
     @pl.when(me == 0)
     def _():
-        for d in range(1, GROUP):
-            remote(piece, gout.at[pl.ds(d * PIECE, PIECE)], r3s.at[0], r3r.at[d], d).wait_recv()
-        att[0:NG] = gout[...]
+        for h in range(2):
+            for d in range(1, GROUP):
+                remote(
+                    piece.at[h], gout.at[h, pl.ds(d * PIECE, PIECE)], r3s.at[h], r3r.at[h, d], d
+                ).wait_recv()
+            att[0:NG, h * wide : (h + 1) * wide] = gout[h]
 
     finish(0)
 
@@ -398,24 +405,28 @@
 
         @pl.when(j > 0)
         def _():
-            deliver.wait_send()
+            for h in range(2):
+                deliver(h).wait_send()
 
     @pl.when(g > 0)
     def _():
-        raise_up.wait_send()
+        for h in range(2):
+            raise_up(h).wait_send()
 
     for d in range(1, GROUP):
         @pl.when((g > 0) | ((j + d) % GROUP != 0))
         def _():
             gather(d).wait_send()
 
-        spread(d).wait_send()
+        for h in range(2):
+            spread(h, d).wait_send()
 
 
 def shards(n, tokens, w_query, w_key, w_value, w_out, ln_gain, ln_bias):
     rows, width = tokens.shape
     groups = n // GROUP
     ext = rows + 2 * BLOCK + NG
+    wide = width // 2
     dma = pltpu.SemaphoreType.DMA
     weight = pltpu.VMEM((width, width), BF16)
     scratch = [
@@ -428,21 +439,20 @@
         pltpu.VMEM((ext, width), BF16),
         pltpu.VMEM((2 * NG, width), BF16),
         pltpu.VMEM((rows // NG, 2 * NG, NG + 2 * BLOCK), F32),
-        pltpu.VMEM((NG, width + LANES), BF16),
-        pltpu.VMEM((NG, LANES), F32),
-        pltpu.VMEM((GROUP, PIECE, width + LANES), BF16),
-        pltpu.VMEM((1, PIECE, width + LANES), BF16),
-        pltpu.VMEM((groups, PIECE, width + LANES), BF16),
-        pltpu.VMEM((PIECE, width), BF16),
-        pltpu.VMEM((NG, width), BF16),
+        pltpu.VMEM((2, NG, wide + LANES), BF16),
+        pltpu.VMEM((2, GROUP, PIECE, wide + LANES), BF16),
+        pltpu.VMEM((2, PIECE, wide + LANES), BF16),
+        pltpu.VMEM((2, groups, PIECE, wide + LANES), BF16),
+        pltpu.VMEM((2, PIECE, wide), BF16),
+        pltpu.VMEM((2, NG, wide), BF16),
         pltpu.VMEM((rows, width), BF16),
         dma((8,)), dma((2,)), dma((2,)),
         dma((GROUP,)), dma((1,)),
         dma((groups,)), dma((1,)),
         dma((GROUP,)), dma((GROUP,)),
-        dma((GROUP,)), dma((GROUP,)),
-        dma((1,)), dma((groups,)),
-        dma((1,)), dma((GROUP,)),
+        dma((2, GROUP)), dma((2, GROUP)),
+        dma((2,)), dma((2, groups)),
+        dma((2,)), dma((2, GROUP)),
     ]
     anywhere = pl.BlockSpec(memory_space=pl.ANY)
     vmem = pl.BlockSpec(memory_space=pltpu.VMEM)

time: 38.5 us -> 36.9 us (0.958)
  Pallas kernels: 36.6 us -> 34.9 us
    pallas_call x1, Pallas kernels: 36.6 us -> 34.9 us  [shards(): pl.pallas_call(functools.partial(kernel, n), out_shape=jax.ShapeDtypeStru...]
where the time goes in v3:
time: 36.9 us; the launch traced here: 36.7 us
  Pallas kernels  34.9 us (95%)
  local copies, waits for them, and re-layouts  1.77 us (5%)
    pallas_call x1, Pallas kernels, shards(): pl.pallas_call(functools.partial(kernel, n), out_shape=jax.ShapeDtypeStru...  34.9 us
    unnamed x1, local copies, waits for them, and re-layouts  1.77 us

profile of v3, /device:TPU:0, one launch (start us, length us, event | category | flops | bytes accessed | tf_op | source)
XLA Modules:
  0.0 36.7 jit_solution(645164002792081803)
XLA Ops:
  0.0 34.9 %shard_map.73 = bf16[256,768]{1,0:T(8,128)(2,1)} custom-call(bf16[256,768]{1,0:T(8,128)(2,1)} %tok_in.1, bf16[768,768]{1,0:T(8,128)(2,1)} %wq_in.1, bf16[768,768]{1,0:T(8,128)(2,1)} %wk_in.1, bf16[768,768]{1,0:T(8,128)(2,1)} %wv_in.1, bf16[768,768]{1,0:T(8,128)(2,1)} %wo_in.1, f32[768]{0:T(1024)} %gain_in.1, f32[768]{0:T(1024)} %bias_in.1), custom_call_target="tpu_custom_call" | custom-call | tf_op jit(solution)/shard_map/pallas_call | solution.py:459
  34.9 1.8 %copy.9 = bf16[256,768]{1,0:T(8,128)(2,1)} copy(bf16[256,768]{1,0:T(8,128)(2,1)} %shard_map.73) | data formatting | bytes 786432

commit v4 on v3

--- a/solution.py
+++ b/solution.py
@@ -35,7 +35,8 @@
     groups = n // GROUP
     scale = 1.0 / math.sqrt(width // H)
     own = BLOCK
-    right_at = BLOCK + rows
+    left_at = rows
+    right_at = rows + BLOCK
     glob = rows + 2 * BLOCK
     me = lax.axis_index("seq")
     g = me // GROUP
@@ -48,7 +49,7 @@
         )
 
     local = [
-        pltpu.make_async_copy(tok_in, tok.at[pl.ds(own, rows)], loc.at[0]),
+        pltpu.make_async_copy(tok_in, tok.at[pl.ds(0, rows)], loc.at[0]),
         pltpu.make_async_copy(wq_in, wq, loc.at[1]),
         pltpu.make_async_copy(wk_in, wk, loc.at[2]),
         pltpu.make_async_copy(wv_in, wv, loc.at[3]),
@@ -115,7 +116,7 @@
 
     to_left = remote(tok_in.at[pl.ds(0, BLOCK)], tok.at[pl.ds(right_at, BLOCK)], halo_s.at[0], halo_r.at[0], me - 1)
     to_right = remote(
-        tok_in.at[pl.ds(rows - BLOCK, BLOCK)], tok.at[pl.ds(0, BLOCK)], halo_s.at[1], halo_r.at[1], me + 1
+        tok_in.at[pl.ds(rows - BLOCK, BLOCK)], tok.at[pl.ds(left_at, BLOCK)], halo_s.at[1], halo_r.at[1], me + 1
     )
 
     @pl.when(has_left)
@@ -131,7 +132,7 @@
 
     @pl.when(me == 0)
     def _():
-        tok[0:BLOCK] = jnp.zeros((BLOCK, width), BF16)
+        tok[left_at : left_at + BLOCK] = jnp.zeros((BLOCK, width), BF16)
 
     @pl.when(me == n - 1)
     def _():
@@ -139,20 +140,19 @@
 
     tile = 2 * LANES if width % (2 * LANES) == 0 else LANES
 
-    def project(start, count, w, dst):
-        @pl.loop(0, width // tile)
-        def _(t):
-            cols = pl.ds(pl.multiple_of(t * tile, tile), tile)
-            dst[start : start + count, cols] = jnp.dot(
-                tok[start : start + count], w[:, cols], preferred_element_type=F32
-            ).astype(BF16)
+    def project(w, dst, pieces):
+        start, count = pieces[0][0], sum(piece_[2] for piece_ in pieces)
+        for t in range(width // tile):
+            cols = slice(t * tile, (t + 1) * tile)
+            res = jnp.dot(tok[start : start + count], w[:, cols], preferred_element_type=F32).astype(BF16)
+            for src, to, size in pieces:
+                dst[to : to + size, cols] = res[src - start : src - start + size]
 
     def project_query(start, count, dst):
         first_half = lax.broadcasted_iota(jnp.int32, (NG, tile), 1) % LANES < BLOCK
 
-        @pl.loop(0, width // tile)
-        def _(t):
-            cols = pl.ds(pl.multiple_of(t * tile, tile), tile)
+        for t in range(width // tile):
+            cols = slice(t * tile, (t + 1) * tile)
             res = jnp.dot(tok[start : start + count], wq[:, cols], preferred_element_type=F32) * scale
             for c in range(count // NG):
                 part = res[c * NG : (c + 1) * NG]
@@ -161,7 +161,7 @@
 
     local[0].wait()
     local[1].wait()
-    project_query(own, rows, q)
+    project_query(0, rows, q)
 
     def gather_sends():
         for d in range(1, GROUP):
@@ -184,7 +184,7 @@
         gather_sends()
 
     local[2].wait()
-    project(own, rows, wk, k)
+    project(wk, k, [(0, own, rows)])
 
     @pl.when(g > 0)
     def _():
@@ -192,7 +192,7 @@
         gather_sends()
 
     local[3].wait()
-    project(own, rows, wv, v)
+    project(wv, v, [(0, own, rows)])
 
     shape = (2 * NG, NG + 2 * BLOCK)
     row_block = lax.broadcasted_iota(jnp.int32, shape, 0) % NG // BLOCK
@@ -202,18 +202,6 @@
         place = me * rows + (c * NG - BLOCK) + key_id
         ok = (apart >= 0) & (apart <= 2) & (place >= NG) & (place < n * rows)
         mask[c] = jnp.where(ok, 0.0, -jnp.inf).astype(F32)
-
-    @pl.when(has_left)
-    def _():
-        to_right.wait_recv()
-
-    @pl.when(has_right)
-    def _():
-        to_left.wait_recv()
-
-    for w, dst in ((wk, k), (wv, v)):
-        project(0, BLOCK, w, dst)
-        project(right_at, BLOCK, w, dst)
 
     @pl.when(me > 0)
     def _():
@@ -311,16 +299,24 @@
     def finish(c):
         at = slice(c * NG, (c + 1) * NG)
         proj = jnp.dot(att[at], wo[...], preferred_element_type=F32)
-        summed = tok[own + c * NG : own + (c + 1) * NG].astype(F32) + proj
+        summed = tok[c * NG : (c + 1) * NG].astype(F32) + proj
         center = summed - jnp.mean(summed, axis=-1, keepdims=True)
         spread_ = jnp.mean(center * center, axis=-1, keepdims=True)
         out_ref[at] = (center * lax.rsqrt(spread_ + 1e-05) * gain_ref[...][None] + bias_ref[...][None]).astype(BF16)
 
+    @pl.when(has_left)
+    def _():
+        to_right.wait_recv()
+
+    @pl.when(has_right)
+    def _():
+        to_left.wait_recv()
+
     for w, dst in ((wk, k), (wv, v)):
-        project(glob, NG, w, dst)
+        project(w, dst, [(left_at, 0, BLOCK), (right_at, own + rows, BLOCK), (glob, glob, NG)])
 
     last = chunks - 1
-    early = min(4, pairs)
+    early = min(2, pairs)
     windows(last, 0, early)
 
     def raise_up(h):

time: 36.9 us -> 36.2 us (0.981)
  Pallas kernels: 34.9 us -> 34.3 us
    pallas_call x1, Pallas kernels: 34.9 us -> 34.3 us  [shards(): pl.pallas_call(functools.partial(kernel, n), out_shape=jax.ShapeDtypeStru...]
where the time goes in v4:
time: 36.2 us; the launch traced here: 36 us
  Pallas kernels  34.3 us (95%)
  local copies, waits for them, and re-layouts  1.77 us (5%)
    pallas_call x1, Pallas kernels, shards(): pl.pallas_call(functools.partial(kernel, n), out_shape=jax.ShapeDtypeStru...  34.3 us
    unnamed x1, local copies, waits for them, and re-layouts  1.77 us

profile of v4, /device:TPU:0, one launch (start us, length us, event | category | flops | bytes accessed | tf_op | source)
XLA Modules:
  0.0 36.0 jit_solution(3912492025555299134)
XLA Ops:
  0.0 34.3 %shard_map.73 = bf16[256,768]{1,0:T(8,128)(2,1)} custom-call(bf16[256,768]{1,0:T(8,128)(2,1)} %tok_in.1, bf16[768,768]{1,0:T(8,128)(2,1)} %wq_in.1, bf16[768,768]{1,0:T(8,128)(2,1)} %wk_in.1, bf16[768,768]{1,0:T(8,128)(2,1)} %wv_in.1, bf16[768,768]{1,0:T(8,128)(2,1)} %wo_in.1, f32[768]{0:T(1024)} %gain_in.1, f32[768]{0:T(1024)} %bias_in.1), custom_call_target="tpu_custom_call" | custom-call | tf_op jit(solution)/shard_map/pallas_call | solution.py:455
  34.3 1.8 %copy.9 = bf16[256,768]{1,0:T(8,128)(2,1)} copy(bf16[256,768]{1,0:T(8,128)(2,1)} %shard_map.73) | data formatting | bytes 786432

commit v5 on v4

--- a/solution.py
+++ b/solution.py
@@ -27,7 +27,7 @@
     n, tok_in, wq_in, wk_in, wv_in, wo_in, gain_in, bias_in, out_ref,
     tok, wq, wk, wv, wo, gain_ref, bias_ref, q, k, v, qg, mask, pacc, racc, cacc, zacc,
     piece, gout, att,
-    loc, halo_s, halo_r, s1s, s1r, s2s, s2r, s3s, s3r, r1s, r1r, r2s, r2r, r3s, r3r,
+    loc, halo_s, halo_r, s1s, s1r, s2s, s2x, s2r, s3s, s3r, r1s, r1r, r2s, r2r, r3s, r3r,
 ):
     rows, width = tok_in.shape
     chunks = rows // NG
@@ -75,7 +75,7 @@
 
     @pl.when(g > 0)
     def _():
-        greet(j)
+        greet(jnp.where(j == 0, 1, j))
 
     has_left = me > 0
     has_right = me < n - 1
@@ -90,21 +90,39 @@
     def _():
         greet(me + 1)
 
-    peers = GROUP - 1 + jnp.where(g == 0, groups - 1, 1) + jnp.where(cross_left, 1, 0) + jnp.where(cross_right, 1, 0)
+    column = jnp.where(j == 0, 0, groups - 1) + jnp.where(j == 1, groups - 1, 0)
+    peers = GROUP - 1 + jnp.where(g == 0, column, 1) + jnp.where(cross_left, 1, 0) + jnp.where(cross_right, 1, 0)
     pl.semaphore_wait(barrier, peers)
 
     def glob_piece(index):
         return tok.at[pl.ds(pl.multiple_of(glob + index * PIECE, PIECE), PIECE)]
 
+    wide = pairs // 2 * LANES
+
     def scatter(d):
-        return remote(tok_in.at[pl.ds(d * PIECE, PIECE)], glob_piece(d), s1s.at[d], s1r.at[0], d)
-
-    def climb(other):
-        return remote(glob_piece(j), glob_piece(j), s2s.at[other], s2r.at[0], other * GROUP + j)
-
-    def gather(d):
+        first, count = (0, 2 * PIECE) if d == 1 else (d * PIECE, PIECE)
+        return remote(
+            tok_in.at[pl.ds(first, count)], tok.at[pl.ds(glob + first, count)], s1s.at[d], s1r.at[0], d
+        )
+
+    def glob_half(index, h):
+        return tok.at[pl.ds(pl.multiple_of(glob + index * PIECE, PIECE), PIECE), pl.ds(h * wide, wide)]
+
+    def climb(other, h):
+        return remote(glob_half(j, h), glob_half(j, h), s2s.at[h, other], s2r.at[h], other * GROUP + j)
+
+    def climb_first(other, h):
+        return remote(glob_half(0, h), glob_half(0, h), s2x.at[h, other], s2r.at[h], other * GROUP)
+
+    def gather(h, d):
         t = (j + d) % GROUP
-        return remote(glob_piece(j), glob_piece(j), s3s.at[d], s3r.at[d], base + t)
+        return remote(glob_half(j, h), glob_half(j, h), s3s.at[h, d], s3r.at[h, d], base + t)
+
+    def gathers(d):
+        wanted = (j + d) % GROUP != 0
+        if d == 1:
+            wanted = wanted & (j > 0)
+        return (g > 0) | wanted
 
     keep = pltpu.make_async_copy(tok_in.at[pl.ds(0, NG)], tok.at[pl.ds(glob, NG)], loc.at[5])
 
@@ -163,33 +181,49 @@
     local[1].wait()
     project_query(0, rows, q)
 
-    def gather_sends():
+    def gather_sends(h):
         for d in range(1, GROUP):
-            @pl.when((g > 0) | ((j + d) % GROUP != 0))
+            @pl.when(gathers(d))
             def _():
-                gather(d).start()
+                gather(h, d).start()
 
     @pl.when(g == 0)
     def _():
-        @pl.when(j > 0)
+        @pl.when(j > 1)
         def _():
             remote(glob_piece(j), glob_piece(j), s1s.at[0], s1r.at[0], 0).wait_recv()
 
+        @pl.when(j == 1)
+        def _():
+            two = tok.at[pl.ds(glob, 2 * PIECE)]
+            remote(two, two, s1s.at[0], s1r.at[0], 0).wait_recv()
+
         @pl.when(j == 0)
         def _():
             keep.wait()
 
-        for other in range(1, groups):
-            climb(other).start()
-        gather_sends()
+        for h in range(2):
+            @pl.when(j > 0)
+            def _():
+                for other in range(1, groups):
+                    climb(other, h).start()
+
+            @pl.when(j == 1)
+            def _():
+                for other in range(1, groups):
+                    climb_first(other, h).start()
+
+        for h in range(2):
+            gather_sends(h)
 
     local[2].wait()
     project(wk, k, [(0, own, rows)])
 
     @pl.when(g > 0)
     def _():
-        remote(glob_piece(j), glob_piece(j), s2s.at[0], s2r.at[0], j).wait_recv()
-        gather_sends()
+        for h in range(2):
+            remote(glob_half(j, h), glob_half(j, h), s2s.at[h, 0], s2r.at[h], jnp.where(j == 0, 1, j)).wait_recv()
+            gather_sends(h)
 
     local[3].wait()
     project(wv, v, [(0, own, rows)])
@@ -203,11 +237,12 @@
         ok = (apart >= 0) & (apart <= 2) & (place >= NG) & (place < n * rows)
         mask[c] = jnp.where(ok, 0.0, -jnp.inf).astype(F32)
 
-    @pl.when(me > 0)
-    def _():
-        for d in range(1, GROUP):
+    for d in range(1, GROUP):
+        @pl.when(me > (1 if d == 1 else 0))
+        def _():
             t = (j + GROUP - d) % GROUP
-            remote(glob_piece(t), glob_piece(t), s3s.at[d], s3r.at[d], base + t).wait_recv()
+            for h in range(2):
+                remote(glob_half(t, h), glob_half(t, h), s3s.at[h, d], s3r.at[h, d], base + t).wait_recv()
 
     project_query(glob, NG, qg)
 
@@ -230,7 +265,6 @@
         return pl.ds(pl.multiple_of(index * PIECE, PIECE), PIECE)
 
     hp = pairs // 2
-    wide = hp * LANES
 
     def spread(h, d):
         t = (j + d) % GROUP
@@ -396,23 +430,29 @@
 
     @pl.when(g == 0)
     def _():
-        for other in range(1, groups):
-            climb(other).wait_send()
-
         @pl.when(j > 0)
         def _():
             for h in range(2):
+                for other in range(1, groups):
+                    climb(other, h).wait_send()
                 deliver(h).wait_send()
 
+        @pl.when(j == 1)
+        def _():
+            for h in range(2):
+                for other in range(1, groups):
+                    climb_first(other, h).wait_send()
+
     @pl.when(g > 0)
     def _():
         for h in range(2):
             raise_up(h).wait_send()
 
     for d in range(1, GROUP):
-        @pl.when((g > 0) | ((j + d) % GROUP != 0))
-        def _():
-            gather(d).wait_send()
+        @pl.when(gathers(d))
+        def _():
+            for h in range(2):
+                gather(h, d).wait_send()
 
         for h in range(2):
             spread(h, d).wait_send()
@@ -444,8 +484,8 @@
         pltpu.VMEM((rows, width), BF16),
         dma((8,)), dma((2,)), dma((2,)),
         dma((GROUP,)), dma((1,)),
-        dma((groups,)), dma((1,)),
-        dma((GROUP,)), dma((GROUP,)),
+        dma((2, groups)), dma((2, groups)), dma((2,)),
+        dma((2, GROUP)), dma((2, GROUP)),
         dma((2, GROUP)), dma((2, GROUP)),
         dma((2,)), dma((2, groups)),
         dma((2,)), dma((2, GROUP)),

time: 36.2 us -> 34.1 us (0.942)
  Pallas kernels: 34.3 us -> 32.1 us
    pallas_call x1, Pallas kernels: 34.3 us -> 32.1 us  [shards(): pl.pallas_call(functools.partial(kernel, n), out_shape=jax.ShapeDtypeStru...]
where the time goes in v5:
time: 34.1 us; the launch traced here: 33.9 us
  Pallas kernels  32.1 us (94%)
  local copies, waits for them, and re-layouts  1.77 us (5%)
    pallas_call x1, Pallas kernels, shards(): pl.pallas_call(functools.partial(kernel, n), out_shape=jax.ShapeDtypeStru...  32.1 us
    unnamed x1, local copies, waits for them, and re-layouts  1.77 us

profile of v5, /device:TPU:0, one launch (start us, length us, event | category | flops | bytes accessed | tf_op | source)
XLA Modules:
  0.0 33.9 jit_solution(12528295415391428374)
XLA Ops:
  0.0 32.1 %shard_map.73 = bf16[256,768]{1,0:T(8,128)(2,1)} custom-call(bf16[256,768]{1,0:T(8,128)(2,1)} %tok_in.1, bf16[768,768]{1,0:T(8,128)(2,1)} %wq_in.1, bf16[768,768]{1,0:T(8,128)(2,1)} %wk_in.1, bf16[768,768]{1,0:T(8,128)(2,1)} %wv_in.1, bf16[768,768]{1,0:T(8,128)(2,1)} %wo_in.1, f32[768]{0:T(1024)} %gain_in.1, f32[768]{0:T(1024)} %bias_in.1), custom_call_target="tpu_custom_call" | custom-call | tf_op jit(solution)/shard_map/pallas_call | solution.py:495
  32.2 1.8 %copy.9 = bf16[256,768]{1,0:T(8,128)(2,1)} copy(bf16[256,768]{1,0:T(8,128)(2,1)} %shard_map.73) | data formatting | bytes 786432

commit v6 on v5

--- a/solution.py
+++ b/solution.py
@@ -177,10 +177,6 @@
                 dst[2 * c * NG : (2 * c + 1) * NG, cols] = jnp.where(first_half, part, 0.0).astype(BF16)
                 dst[(2 * c + 1) * NG : (2 * c + 2) * NG, cols] = jnp.where(first_half, 0.0, part).astype(BF16)
 
-    local[0].wait()
-    local[1].wait()
-    project_query(0, rows, q)
-
     def gather_sends(h):
         for d in range(1, GROUP):
             @pl.when(gathers(d))
@@ -216,6 +212,9 @@
         for h in range(2):
             gather_sends(h)
 
+    local[0].wait()
+    local[1].wait()
+    project_query(0, rows, q)
     local[2].wait()
     project(wk, k, [(0, own, rows)])
 
@@ -331,8 +330,10 @@
             window(c, p + 1)
 
     def finish(c):
+        normalize(c, jnp.dot(att[c * NG : (c + 1) * NG], wo[...], preferred_element_type=F32))
+
+    def normalize(c, proj):
         at = slice(c * NG, (c + 1) * NG)
-        proj = jnp.dot(att[at], wo[...], preferred_element_type=F32)
         summed = tok[c * NG : (c + 1) * NG].astype(F32) + proj
         center = summed - jnp.mean(summed, axis=-1, keepdims=True)
         spread_ = jnp.mean(center * center, axis=-1, keepdims=True)
@@ -349,9 +350,6 @@
     for w, dst in ((wk, k), (wv, v)):
         project(w, dst, [(left_at, 0, BLOCK), (right_at, own + rows, BLOCK), (glob, glob, NG)])
 
-    last = chunks - 1
-    early = min(2, pairs)
-    windows(last, 0, early)
 
     def raise_up(h):
         return remote(cacc.at[h], zacc.at[h, g], r2s.at[h], r2r.at[h, g], j)
@@ -373,8 +371,7 @@
                 cacc[h, :, p * LANES : (p + 1) * LANES] = sent[p]
             raise_up(h).start()
 
-    windows(last, early, pairs)
-    for c in range(last):
+    for c in range(chunks):
         windows(c, 0, pairs)
 
     def deliver(h):
@@ -406,14 +403,18 @@
 
     @pl.when(me == 0)
     def _():
+        proj = jnp.zeros((NG, width), F32)
         for h in range(2):
             for d in range(1, GROUP):
                 remote(
                     piece.at[h], gout.at[h, pl.ds(d * PIECE, PIECE)], r3s.at[h], r3r.at[h, d], d
                 ).wait_recv()
-            att[0:NG, h * wide : (h + 1) * wide] = gout[h]
-
-    finish(0)
+            proj += jnp.dot(gout[h], wo[h * wide : (h + 1) * wide], preferred_element_type=F32)
+        normalize(0, proj)
+
+    @pl.when(me > 0)
+    def _():
+        finish(0)
 
     @pl.when(has_left)
     def _():

time: 34.1 us -> 34.1 us (level)
  no operation moved by 1% of the time
where the time goes in v6:
time: 34.1 us; the launch traced here: 33.9 us
  Pallas kernels  32.1 us (94%)
  local copies, waits for them, and re-layouts  1.77 us (5%)
    pallas_call x1, Pallas kernels, shards(): pl.pallas_call(functools.partial(kernel, n), out_shape=jax.ShapeDtypeStru...  32.1 us
    unnamed x1, local copies, waits for them, and re-layouts  1.77 us

profile of v6, /device:TPU:0, one launch (start us, length us, event | category | flops | bytes accessed | tf_op | source)
XLA Modules:
  0.0 33.9 jit_solution(10946885927769180840)
XLA Ops:
  0.0 32.1 %shard_map.73 = bf16[256,768]{1,0:T(8,128)(2,1)} custom-call(bf16[256,768]{1,0:T(8,128)(2,1)} %tok_in.1, bf16[768,768]{1,0:T(8,128)(2,1)} %wq_in.1, bf16[768,768]{1,0:T(8,128)(2,1)} %wk_in.1, bf16[768,768]{1,0:T(8,128)(2,1)} %wv_in.1, bf16[768,768]{1,0:T(8,128)(2,1)} %wo_in.1, f32[768]{0:T(1024)} %gain_in.1, f32[768]{0:T(1024)} %bias_in.1), custom_call_target="tpu_custom_call" | custom-call | tf_op jit(solution)/shard_map/pallas_call | solution.py:496
  32.1 1.8 %copy.9 = bf16[256,768]{1,0:T(8,128)(2,1)} copy(bf16[256,768]{1,0:T(8,128)(2,1)} %shard_map.73) | data formatting | bytes 786432
